TPU v7x, 32 devices: a whole 2x2x4 slice. The times are simulated.
32 devices in a mesh: seq: 8 (over z, x), tp: 4 (over y, core).
Axes of the slice: x: 2, y: 2, z: 4, core: 2. Of those that a mesh axis runs over, the one named last changes fastest.
Arguments:
- tokens: bfloat16 [16384, 1024], P('seq'), may hold values from -6 to 6
- cotangent: bfloat16 [16384, 1024], P('seq'), may hold values from -6 to 6
- start_flags: int32 [8], P('seq'), may hold values from 0 to 1, as said below
- gain_mixer: float32 [1024], replicated, may hold values from 0.5 to 1.5
- w_bgate: bfloat16 [1024, 1024], P(None, 'tp'), may hold values from -0.1875 to 0.1875
- w_cgate: bfloat16 [1024, 1024], P(None, 'tp'), may hold values from -0.1875 to 0.1875
- w_input: bfloat16 [1024, 1024], P(None, 'tp'), may hold values from -0.1875 to 0.1875
- conv_kernel: bfloat16 [3, 1024], P(None, 'tp'), may hold values from -3.5 to 3.5
- w_output: bfloat16 [1024, 1024], P('tp'), may hold values from -0.1875 to 0.1875
- gain_ffn: float32 [1024], replicated, may hold values from 0.5 to 1.5
- w_gate: bfloat16 [1024, 4608], P(None, 'tp'), may hold values from -0.1875 to 0.1875
- w_up: bfloat16 [1024, 4608], P(None, 'tp'), may hold values from -0.1875 to 0.1875
- w_down: bfloat16 [4608, 1024], P('tp'), may hold values from -0.09375 to 0.09375
- mean_gain_mixer: float32 [1024], replicated, may hold values from -16 to 16
- square_gain_mixer: float32 [1024], replicated, may hold values from 1 to 100
- mean_w_bgate: float32 [1024, 1024], P('seq', 'tp'), may hold values from -16 to 16
- square_w_bgate: float32 [1024, 1024], P('seq', 'tp'), may hold values from 1 to 100
- mean_w_cgate: float32 [1024, 1024], P('seq', 'tp'), may hold values from -16 to 16
- square_w_cgate: float32 [1024, 1024], P('seq', 'tp'), may hold values from 1 to 100
- mean_w_input: float32 [1024, 1024], P('seq', 'tp'), may hold values from -16 to 16
- square_w_input: float32 [1024, 1024], P('seq', 'tp'), may hold values from 1 to 100
- mean_conv_kernel: float32 [3, 1024], P(None, 'tp'), may hold values from -16 to 16
- square_conv_kernel: float32 [3, 1024], P(None, 'tp'), may hold values from 1 to 100
- mean_w_output: float32 [1024, 1024], P('tp', 'seq'), may hold values from -16 to 16
- square_w_output: float32 [1024, 1024], P('tp', 'seq'), may hold values from 1 to 100
- mean_gain_ffn: float32 [1024], replicated, may hold values from -16 to 16
- square_gain_ffn: float32 [1024], replicated, may hold values from 1 to 100
- mean_w_gate: float32 [1024, 4608], P('seq', 'tp'), may hold values from -16 to 16
- square_w_gate: float32 [1024, 4608], P('seq', 'tp'), may hold values from 1 to 100
- mean_w_up: float32 [1024, 4608], P('seq', 'tp'), may hold values from -16 to 16
- square_w_up: float32 [1024, 4608], P('seq', 'tp'), may hold values from 1 to 100
- mean_w_down: float32 [4608, 1024], P('tp', 'seq'), may hold values from -16 to 16
- square_w_down: float32 [4608, 1024], P('tp', 'seq'), may hold values from 1 to 100
Outputs:
- block_out: bfloat16 [16384, 1024], P('seq')
- grad_tokens: float32 [16384, 1024], P('seq')
- grad_gain_mixer: float32 [1024], replicated
- next_gain_mixer: float32 [1024], replicated
- mean_next_gain_mixer: float32 [1024], replicated
- square_next_gain_mixer: float32 [1024], replicated
- grad_w_bgate: float32 [1024, 1024], P('seq', 'tp')
- next_w_bgate: float32 [1024, 1024], P('seq', 'tp')
- mean_next_w_bgate: float32 [1024, 1024], P('seq', 'tp')
- square_next_w_bgate: float32 [1024, 1024], P('seq', 'tp')
- grad_w_cgate: float32 [1024, 1024], P('seq', 'tp')
- next_w_cgate: float32 [1024, 1024], P('seq', 'tp')
- mean_next_w_cgate: float32 [1024, 1024], P('seq', 'tp')
- square_next_w_cgate: float32 [1024, 1024], P('seq', 'tp')
- grad_w_input: float32 [1024, 1024], P('seq', 'tp')
- next_w_input: float32 [1024, 1024], P('seq', 'tp')
- mean_next_w_input: float32 [1024, 1024], P('seq', 'tp')
- square_next_w_input: float32 [1024, 1024], P('seq', 'tp')
- grad_conv_kernel: float32 [3, 1024], P(None, 'tp')
- next_conv_kernel: float32 [3, 1024], P(None, 'tp')
- mean_next_conv_kernel: float32 [3, 1024], P(None, 'tp')
- square_next_conv_kernel: float32 [3, 1024], P(None, 'tp')
- grad_w_output: float32 [1024, 1024], P('tp', 'seq')
- next_w_output: float32 [1024, 1024], P('tp', 'seq')
- mean_next_w_output: float32 [1024, 1024], P('tp', 'seq')
- square_next_w_output: float32 [1024, 1024], P('tp', 'seq')
- grad_gain_ffn: float32 [1024], replicated
- next_gain_ffn: float32 [1024], replicated
- mean_next_gain_ffn: float32 [1024], replicated
- square_next_gain_ffn: float32 [1024], replicated
- grad_w_gate: float32 [1024, 4608], P('seq', 'tp')
- next_w_gate: float32 [1024, 4608], P('seq', 'tp')
- mean_next_w_gate: float32 [1024, 4608], P('seq', 'tp')
- square_next_w_gate: float32 [1024, 4608], P('seq', 'tp')
- grad_w_up: float32 [1024, 4608], P('seq', 'tp')
- next_w_up: float32 [1024, 4608], P('seq', 'tp')
- mean_next_w_up: float32 [1024, 4608], P('seq', 'tp')
- square_next_w_up: float32 [1024, 4608], P('seq', 'tp')
- grad_w_down: float32 [4608, 1024], P('tp', 'seq')
- next_w_down: float32 [4608, 1024], P('tp', 'seq')
- mean_next_w_down: float32 [4608, 1024], P('tp', 'seq')
- square_next_w_down: float32 [4608, 1024], P('tp', 'seq')
Inputs may be any that keep to these rules, and one draw needn't show every extreme that they name: `start_flags`: the first shard's flag is 1; shards 1 and 5 have flag 0, so they continue the sequence of the shard before them.
All inputs are finite; a program needn't handle non-finite values.
Results may differ from a plain program's by a relative error of at most 0.0075.
The roundings to bfloat16 on the way count: a program that leaves them out, or rounds other values in their place, can miss the bound.
Values sent between devices are 32-bit elements; how exact they have to be, the bound alone decides.
No kernel may reach another device: no remote copies, remote signals or barrier semaphores. Data moves between devices by JAX's collectives and lax.ppermute only.
A program may use at most 192 MiB of HBM per device.

v0:
```python
import jax
import jax.numpy as jnp
from jax import lax
from jax.sharding import PartitionSpec as P

EPS = 1e-05


def shifted(block, axis, distance):
    devices = range(lax.axis_size(axis))
    route = [(i - distance, i) for i in devices if i - distance in devices]
    return lax.ppermute(block, axis, route)


def inner_rows(left, right):
    return lax.dot_general(
        left, right, (((0,), (0,)), ((), ())), preferred_element_type=jnp.float32
    )


def times_back(left, right):
    return lax.dot_general(
        left, right, (((1,), (1,)), ((), ())), preferred_element_type=jnp.float32
    )


def adamw(weight, grad, mean, square, decay, rate):
    mean_new = 0.9 * mean + 0.1 * grad
    square_new = 0.95 * square + 0.05 * grad * grad
    mean_hat = mean_new / (1.0 - 0.9**3)
    square_hat = square_new / (1.0 - 0.95**3)
    weight_new = weight - rate * (mean_hat / (jnp.sqrt(square_hat) + 1e-08) + decay * weight)
    return (weight_new, mean_new, square_new)


def norm_back(dnormed, normed, inverse):
    return inverse * (dnormed - normed * jnp.mean(dnormed * normed, axis=-1, keepdims=True))


def body(
    tokens,
    cotangent,
    start_flags,
    gain_mixer,
    w_bgate,
    w_cgate,
    w_input,
    conv_kernel,
    w_output,
    gain_ffn,
    w_gate,
    w_up,
    w_down,
    mean_gain_mixer,
    square_gain_mixer,
    mean_w_bgate,
    square_w_bgate,
    mean_w_cgate,
    square_w_cgate,
    mean_w_input,
    square_w_input,
    mean_conv_kernel,
    square_conv_kernel,
    mean_w_output,
    square_w_output,
    mean_gain_ffn,
    square_gain_ffn,
    mean_w_gate,
    square_w_gate,
    mean_w_up,
    square_w_up,
    mean_w_down,
    square_w_down,
):
    count = tokens.shape[0]
    xin = tokens.astype(jnp.float32)
    inverse_one = lax.rsqrt(jnp.mean(xin * xin, axis=-1, keepdims=True) + EPS)
    norm_one = xin * inverse_one
    hone = (norm_one * gain_mixer).astype(jnp.bfloat16)
    bgate = jnp.dot(hone, w_bgate, preferred_element_type=jnp.float32)
    cgate = jnp.dot(hone, w_cgate, preferred_element_type=jnp.float32)
    xval = jnp.dot(hone, w_input, preferred_element_type=jnp.float32)
    mixed_in = bgate * xval
    keeper = (1 - start_flags[0]).astype(jnp.float32)
    kernel = conv_kernel.astype(jnp.float32)
    previous = shifted(mixed_in[-2:], "seq", 1) * keeper
    extended = jnp.concatenate([previous, mixed_in], axis=0)
    conv = kernel[2] * mixed_in + kernel[1] * extended[1:-1] + kernel[0] * extended[:-2]
    gated = (cgate * conv).astype(jnp.bfloat16)
    mix = lax.psum(jnp.dot(gated, w_output, preferred_element_type=jnp.float32), "tp")
    resid = xin + mix
    inverse_two = lax.rsqrt(jnp.mean(resid * resid, axis=-1, keepdims=True) + EPS)
    norm_two = resid * inverse_two
    htwo = (norm_two * gain_ffn).astype(jnp.bfloat16)
    gate = jnp.dot(htwo, w_gate, preferred_element_type=jnp.float32)
    upval = jnp.dot(htwo, w_up, preferred_element_type=jnp.float32)
    sigma = jax.nn.sigmoid(gate)
    silu_gate = gate * sigma
    act = (silu_gate * upval).astype(jnp.bfloat16)
    ffn = lax.psum(jnp.dot(act, w_down, preferred_element_type=jnp.float32), "tp")
    block_out = (resid + ffn).astype(jnp.bfloat16)
    gout = cotangent.astype(jnp.float32)
    grad_down = inner_rows(act, cotangent)
    dact = times_back(cotangent, w_down)
    dgate = (dact * upval * (sigma * (1.0 + gate * (1.0 - sigma)))).astype(jnp.bfloat16)
    dupval = (dact * silu_gate).astype(jnp.bfloat16)
    grad_gate = inner_rows(htwo, dgate)
    grad_upw = inner_rows(htwo, dupval)
    dhtwo_part = times_back(dgate, w_gate) + times_back(dupval, w_up)
    dhtwo = lax.psum(dhtwo_part, "tp")
    dgain_ffn = jnp.sum(dhtwo * norm_two, axis=0)
    dresid = gout + norm_back(dhtwo * gain_ffn, norm_two, inverse_two)
    dmix = dresid.astype(jnp.bfloat16)
    grad_outw = inner_rows(gated, dmix)
    dgated = times_back(dmix, w_output)
    dcgate = (dgated * conv).astype(jnp.bfloat16)
    dconv = dgated * cgate
    dkernel = jnp.stack(
        [
            jnp.sum(dconv * extended[:-2], axis=0),
            jnp.sum(dconv * extended[1:-1], axis=0),
            jnp.sum(dconv * mixed_in, axis=0),
        ],
        axis=0,
    )
    dextended = (
        jnp.pad(kernel[2] * dconv, ((2, 0), (0, 0)))
        + jnp.pad(kernel[1] * dconv, ((1, 1), (0, 0)))
        + jnp.pad(kernel[0] * dconv, ((0, 2), (0, 0)))
    )
    returned = shifted(dextended[:2] * keeper, "seq", -1)
    dmixed = dextended[2:] + jnp.pad(returned, ((count - 2, 0), (0, 0)))
    dbgate = (dmixed * xval).astype(jnp.bfloat16)
    dxval = (dmixed * bgate).astype(jnp.bfloat16)
    grad_bw = inner_rows(hone, dbgate)
    grad_cw = inner_rows(hone, dcgate)
    grad_xw = inner_rows(hone, dxval)
    shared = (
        lax.psum_scatter(grad_bw, "seq", scatter_dimension=0, tiled=True),
        lax.psum_scatter(grad_cw, "seq", scatter_dimension=0, tiled=True),
        lax.psum_scatter(grad_xw, "seq", scatter_dimension=0, tiled=True),
        lax.psum_scatter(grad_outw, "seq", scatter_dimension=1, tiled=True),
        lax.psum_scatter(grad_gate, "seq", scatter_dimension=0, tiled=True),
        lax.psum_scatter(grad_upw, "seq", scatter_dimension=0, tiled=True),
        lax.psum_scatter(grad_down, "seq", scatter_dimension=1, tiled=True),
    )
    dhone_part = (
        times_back(dbgate, w_bgate) + times_back(dcgate, w_cgate) + times_back(dxval, w_input)
    )
    dhone = lax.psum(dhone_part, "tp")
    dgain_mixer = jnp.sum(dhone * norm_one, axis=0)
    grad_tokens = dresid + norm_back(dhone * gain_mixer, norm_one, inverse_one)
    small = lax.psum((dgain_mixer, dgain_ffn, dkernel), "seq")
    width = w_bgate.shape[0] // lax.axis_size("seq")
    offset = lax.axis_index("seq") * width

    def rows_of(weight):
        return lax.dynamic_slice_in_dim(weight, offset, width, 0).astype(jnp.float32)

    def columns_of(weight):
        return lax.dynamic_slice_in_dim(weight, offset, width, 1).astype(jnp.float32)

    params = [
        gain_mixer,
        rows_of(w_bgate),
        rows_of(w_cgate),
        rows_of(w_input),
        kernel,
        columns_of(w_output),
        gain_ffn,
        rows_of(w_gate),
        rows_of(w_up),
        columns_of(w_down),
    ]
    grads = [
        small[0],
        shared[0],
        shared[1],
        shared[2],
        small[2],
        shared[3],
        small[1],
        shared[4],
        shared[5],
        shared[6],
    ]
    moments = [
        (mean_gain_mixer, square_gain_mixer),
        (mean_w_bgate, square_w_bgate),
        (mean_w_cgate, square_w_cgate),
        (mean_w_input, square_w_input),
        (mean_conv_kernel, square_conv_kernel),
        (mean_w_output, square_w_output),
        (mean_gain_ffn, square_gain_ffn),
        (mean_w_gate, square_w_gate),
        (mean_w_up, square_w_up),
        (mean_w_down, square_w_down),
    ]
    decays = [0.0, 0.1, 0.1, 0.1, 0.1, 0.1, 0.0, 0.1, 0.1, 0.1]
    rates = [0.2, 0.01, 0.01, 0.01, 0.2, 0.01, 0.2, 0.01, 0.01, 0.01]
    outs = [block_out, grad_tokens]
    for index in range(10):
        weight_new, mean_new, square_new = adamw(
            params[index],
            grads[index],
            moments[index][0],
            moments[index][1],
            decays[index],
            rates[index],
        )
        outs = outs + [grads[index], weight_new, mean_new, square_new]
    return tuple(outs)


def solution(mesh):
    in_specs = (
        P("seq", None),
        P("seq", None),
        P("seq"),
        P(),
        P(None, "tp"),
        P(None, "tp"),
        P(None, "tp"),
        P(None, "tp"),
        P("tp", None),
        P(),
        P(None, "tp"),
        P(None, "tp"),
        P("tp", None),
        P(),
        P(),
        P("seq", "tp"),
        P("seq", "tp"),
        P("seq", "tp"),
        P("seq", "tp"),
        P("seq", "tp"),
        P("seq", "tp"),
        P(None, "tp"),
        P(None, "tp"),
        P("tp", "seq"),
        P("tp", "seq"),
        P(),
        P(),
        P("seq", "tp"),
        P("seq", "tp"),
        P("seq", "tp"),
        P("seq", "tp"),
        P("tp", "seq"),
        P("tp", "seq"),
    )
    out_specs = (
        P("seq", None),
        P("seq", None),
        P(),
        P(),
        P(),
        P(),
        P("seq", "tp"),
        P("seq", "tp"),
        P("seq", "tp"),
        P("seq", "tp"),
        P("seq", "tp"),
        P("seq", "tp"),
        P("seq", "tp"),
        P("seq", "tp"),
        P("seq", "tp"),
        P("seq", "tp"),
        P("seq", "tp"),
        P("seq", "tp"),
        P(None, "tp"),
        P(None, "tp"),
        P(None, "tp"),
        P(None, "tp"),
        P("tp", "seq"),
        P("tp", "seq"),
        P("tp", "seq"),
        P("tp", "seq"),
        P(),
        P(),
        P(),
        P(),
        P("seq", "tp"),
        P("seq", "tp"),
        P("seq", "tp"),
        P("seq", "tp"),
        P("seq", "tp"),
        P("seq", "tp"),
        P("seq", "tp"),
        P("seq", "tp"),
        P("tp", "seq"),
        P("tp", "seq"),
        P("tp", "seq"),
        P("tp", "seq"),
    )
    return jax.shard_map(body, mesh=mesh, in_specs=in_specs, out_specs=out_specs, check_vma=False)
```

profile of v0, /device:TPU:0, one launch (start us, length us, event | category | flops | bytes accessed | tf_op | source)
XLA Modules:
  0.0 1340.2 jit_solution(14432429471371438521)
XLA Ops:
  7.3 3.2 fusion.11
  10.5 0.6 copy-done.32
  11.1 1.1 fusion.5
  12.3 1.3 fusion.53
  13.7 2.6 fusion.52
  16.3 4.8 collective-permute-start
  21.9 0.6 collective-permute-done
  22.5 3.5 multiply_convert_fusion.7
  26.0 4.7 fusion.54
  31.0 154.8 %all-reduce.10.cloned.1.call-done = f32[2048,1024]{1,0:T(8,128)} async-done(((f32[2048,1024]{1,0:T(8,128)}), f32[2048,1024]{1,0:T(8,128)}) %all-reduce.10.cloned.1.call-update) | async-done | bytes 8388624 | tf_op jit(solution)/shard_map/psum | solution.py:90
  185.8 5.7 multiply_reduce_fusion.2
  191.6 0.9 multiply_convert_fusion.3
  192.4 2.7 copy-done
  195.2 7.9 fusion.56
  203.1 7.9 fusion.55
  211.0 17.9 %multiply_convert_fusion = (bf16[2048,1152]{1,0:T(8,128)(2,1)}, bf16[2048,1152]{1,0:T(8,128)(2,1)}, bf16[2048,1152]{1,0:T(8,128)(2,1)}) fusion(f32[2048,1152]{1,0:T(8,128)} %fusion.55, f32[2048,1152]{1,0:T(8,128)} %fusion.56, bf16[2048,1024]{1,0:T(8,128)(2,1)} %param.34, bf16[1152,1024]{1,0:T(8,128)(2,1)} %param.45), kind=kOutput, calls=%fused_computation.7 | convolution fusion | flops 4867227648 | bytes 39583744 | tf_op jit(solution)/shard_map/dot_general | solution.py:22
  228.9 7.7 fusion.58
  236.6 8.5 convolution_add_fusion
  245.1 153.1 %all-reduce.12.cloned.1.call-done = f32[2048,1024]{1,0:T(8,128)} async-done(((f32[2048,1024]{1,0:T(8,128)}), f32[2048,1024]{1,0:T(8,128)}) %all-reduce.12.cloned.1.call-update) | async-done | bytes 8388624 | tf_op jit(solution)/shard_map/psum | solution.py:110
  398.3 7.1 multiply_reduce_fusion
  405.3 1.1 copy-done.4
  406.5 1.2 copy-done.12
  407.7 4.5 multiply_add_fusion
  412.2 3.4 copy-done.1
  415.6 2.3 fusion.13
  418.0 4.9 fusion.15
  422.9 2.2 multiply_reduce_fusion.5
  425.1 0.8 copy-done.6
  425.8 2.3 fusion.62
  428.2 0.5 broadcast_multiply_fusion.2
  428.8 2.0 collective-permute-start.1
  430.7 0.4 pad_add_fusion
  431.2 3.4 collective-permute-done.1
  434.5 0.5 multiply_convert_fusion.4
  435.1 1.6 copy-done.7
  436.7 2.2 fusion.63
  439.0 4.5 fusion.61
  443.6 10.3 fusion.64
  454.0 10.3 fusion.65
  464.4 9.7 fusion.66
  474.4 10.2 fusion.57
  484.6 1.3 fusion.60
  485.9 1.3 fusion.59
  487.2 4.7 add_add_fusion
  492.1 0.8 copy-done.28
  492.9 1.8 convert_subtract_fusion.3
  494.7 54.1 %reduce-scatter.10.cloned.1.call-done = f32[128,256]{1,0:T(8,128)} async-done(((f32[1024,256]{1,0:T(8,128)}), f32[128,256]{1,0:T(8,128)}) %reduce-scatter.10.cloned.1.call-update) | async-done | bytes 131088 | tf_op jit(solution)/shard_map/reduce_scatter | solution.py:140
  548.8 1.7 convert_subtract_fusion.5
  550.6 64.6 %reduce-scatter.12.cloned.1.call-done = f32[128,256]{1,0:T(8,128)} async-done(((f32[1024,256]{1,0:T(8,128)}), f32[128,256]{1,0:T(8,128)}) %reduce-scatter.12.cloned.1.call-update) | async-done | bytes 131088 | tf_op jit(solution)/shard_map/reduce_scatter | solution.py:141
  615.2 1.8 convert_subtract_fusion.4
  617.0 65.0 %reduce-scatter.8.cloned.1.call-done = f32[128,256]{1,0:T(8,128)} async-done(((f32[1024,256]{1,0:T(8,128)}), f32[128,256]{1,0:T(8,128)}) %reduce-scatter.8.cloned.1.call-update) | async-done | bytes 131088 | tf_op jit(solution)/shard_map/reduce_scatter | solution.py:139
  681.9 1.9 convert_subtract_fusion.6
  683.8 96.6 %reduce-scatter.16.cloned.1.call-done = f32[128,1152]{1,0:T(8,128)} async-done(((f32[1024,1152]{1,0:T(8,128)}), f32[128,1152]{1,0:T(8,128)}) %reduce-scatter.16.cloned.1.call-update) | async-done | bytes 589840 | tf_op jit(solution)/shard_map/reduce_scatter | solution.py:143
  780.4 2.6 convert_subtract_fusion.2
  783.1 96.6 %reduce-scatter.18.cloned.1.call-done = f32[128,1152]{1,0:T(8,128)} async-done(((f32[1024,1152]{1,0:T(8,128)}), f32[128,1152]{1,0:T(8,128)}) %reduce-scatter.18.cloned.1.call-update) | async-done | bytes 589840 | tf_op jit(solution)/shard_map/reduce_scatter | solution.py:144
  879.7 2.6 convert_subtract_fusion.1
  882.4 97.1 %reduce-scatter.20.cloned.1.call-done = f32[1152,128]{1,0:T(8,128)} async-done(((f32[1152,1024]{1,0:T(8,128)}), f32[1152,128]{1,0:T(8,128)}) %reduce-scatter.20.cloned.1.call-update) | async-done | bytes 589840 | tf_op jit(solution)/shard_map/reduce_scatter | solution.py:145
  979.5 2.8 convert_subtract_fusion
  982.3 288.3 %all-reduce.14.cloned.1.call-done = (f32[2048,1024]{1,0:T(8,128)}, f32[2048,1024]{1,0:T(8,128)}) async-done(((f32[2048,1024]{1,0:T(8,128)}, f32[2048,1024]{1,0:T(8,128)}), (f32[2048,1024]{1,0:T(8,128)}, f32[2048,1024]{1,0:T(8,128)})) %all-reduce.14.cloned.1.call-update) | async-done | bytes 16777232 | tf_op jit(solution)/shard_map/psum | solution.py:100
  1270.7 6.5 fusion.10
  1277.3 17.5 %fusion.9 = (f32[2048,1024]{1,0:T(8,128)}, bf16[2048,1024]{1,0:T(8,128)(2,1)}) fusion(f32[2048,1024]{1,0:T(8,128)} %copy-done.1, bf16[2048,1024]{1,0:T(8,128)(2,1)S(1)} %copy-done.3, f32[2048,1024]{1,0:T(8,128)} %get-tuple-element.53, f32[2048]{0:T(1024)S(1)} %broadcast_multiply_fusion.3, f32[1024]{0:T(1024)S(1)} %copy-done.36, f32[2048]{0:T(1024)S(1)} %copy-done.33, ...), kind=kLoop, calls=%fused_computation.16 | loop fusion | flops 18874368 | bytes 50352128 | tf_op jit(solution)/shard_map/add | solution.py:152
  1294.7 37.1 %all-reduce.4 = (f32[1024]{0:T(1024)S(1)}, f32[3,256]{1,0:T(4,128)S(1)}, f32[1024]{0:T(1024)S(1)}) all-reduce(f32[1024]{0:T(1024)S(1)} %get-tuple-element.44, f32[3,256]{1,0:T(4,128)S(1)} %pad_maximum_fusion.1, f32[1024]{0:T(1024)S(1)} %get-tuple-element.42), channel_id=1, replica_groups=mesh['seq'=8,'tp'=4] {'seq'}, use_global_device_ids=true, to_apply=%region_9.0 | all-reduce | flops 2816 | bytes 22528 | tf_op jit(solution)/shard_map/psum | solution.py:153
  1331.8 0.6 multiply_subtract_fusion.1
  1332.5 0.6 multiply_subtract_fusion
  (128 shorter events, 1.4 us)
Async XLA Ops:
  7.2 3.9 copy-start.35
  7.2 178.6 %all-reduce.10.cloned.1.call-start = ((), (), s32[]{:S(2)}) async-start(), calls=%async_computation.7 | async-start | bytes 16777216 | tf_op jit(solution)/shard_map/psum | solution.py:90
  7.3 3.9 copy-start.2
  11.1 1.1 copy-start.21
  12.3 10.2 copy-start.5
  12.3 1.4 copy-start.15
  13.7 2.6 copy-start.8
  13.7 7.5 copy-start.41
  13.7 8.8 copy-start.19
  16.3 6.1 collective-permute-start
  22.5 3.6 copy-start.14
  30.7 160.8 %copy-start.34 = (f32[1024]{0:T(1024)S(1)}, f32[1024]{0:T(1024)}, u32[]{:S(2)}) copy-start(f32[1024]{0:T(1024)} %param.42) | copy-start | bytes 12292
  30.7 367.5 %all-reduce.12.cloned.1.call-start = ((), (), s32[]{:S(2)}) async-start(), calls=%async_computation.8 | async-start | bytes 16777216 | tf_op jit(solution)/shard_map/psum | solution.py:110
  191.5 3.7 copy-start
  191.6 3.6 copy-start.39
  195.2 7.9 copy-start.13
  195.2 7.9 copy-start.37
  211.0 17.9 %copy-start.38 = (bf16[1024,1152]{1,0:T(8,128)(2,1)S(1)}, bf16[1024,1152]{1,0:T(8,128)(2,1)}, u32[]{:S(2)}) copy-start(bf16[1024,1152]{1,0:T(8,128)(2,1)} %param.43) | copy-start | bytes 7077892
  228.9 7.7 copy-start.40
  228.9 7.7 copy-start.52
  245.1 247.0 %reduce-scatter.14.cloned.1.call-start = ((), (), s32[]{:S(2)}) async-start(), calls=%async_computation.12 | async-start | bytes 1179648 | tf_op jit(solution)/shard_map/reduce_scatter | solution.py:142
  398.3 8.2 copy-start.4
  398.3 9.4 copy-start.12
  412.2 3.4 copy-start.1
  417.9 130.9 %reduce-scatter.10.cloned.1.call-start = ((), (), s32[]{:S(2)}) async-start(), calls=%async_computation.10 | async-start | bytes 1179648 | tf_op jit(solution)/shard_map/reduce_scatter | solution.py:140
  417.9 4.9 copy-start.17
  418.0 4.9 copy-start.18
  422.9 3.0 copy-start.6
  425.8 2.4 copy-start.11
  428.1 187.0 %reduce-scatter.12.cloned.1.call-start = ((), (), s32[]{:S(2)}) async-start(), calls=%async_computation.11 | async-start | bytes 1179648 | tf_op jit(solution)/shard_map/reduce_scatter | solution.py:141
  428.8 5.8 copy-start.9
  428.8 5.8 copy-start.10
  428.8 5.7 collective-permute-start.1
  434.5 2.2 copy-start.7
  439.0 243.0 %reduce-scatter.8.cloned.1.call-start = ((), (), s32[]{:S(2)}) async-start(), calls=%async_computation.9 | async-start | bytes 1179648 | tf_op jit(solution)/shard_map/reduce_scatter | solution.py:139
  443.6 336.9 %reduce-scatter.16.cloned.1.call-start = ((), (), s32[]{:S(2)}) async-start(), calls=%async_computation.13 | async-start | bytes 5308416 | tf_op jit(solution)/shard_map/reduce_scatter | solution.py:143
  453.9 425.8 %reduce-scatter.18.cloned.1.call-start = ((), (), s32[]{:S(2)}) async-start(), calls=%async_computation.14 | async-start | bytes 5308416 | tf_op jit(solution)/shard_map/reduce_scatter | solution.py:144
  464.4 515.1 %reduce-scatter.20.cloned.1.call-start = ((), (), s32[]{:S(2)}) async-start(), calls=%async_computation.15 | async-start | bytes 5308416 | tf_op jit(solution)/shard_map/reduce_scatter | solution.py:145
  474.2 796.5 %all-reduce.14.cloned.1.call-start = ((), (), s32[]{:S(2)}) async-start(), calls=%async_computation.16 | async-start | bytes 33554432 | tf_op jit(solution)/shard_map/psum | solution.py:100
  474.4 10.2 copy-start.20
  484.6 1.3 copy-start.16
  485.9 1.3 copy-start.22
  491.9 0.9 copy-start.28
  491.9 1.0 copy-start.29
  491.9 56.9 %copy-start.30 = (f32[128,256]{1,0:T(8,128)S(1)}, f32[128,256]{1,0:T(8,128)}, u32[]{:S(2)}) copy-start(f32[128,256]{1,0:T(8,128)} %param.50) | copy-start | bytes 393220
  491.9 56.9 %copy-start.31 = (f32[128,256]{1,0:T(8,128)S(1)}, f32[128,256]{1,0:T(8,128)}, u32[]{:S(2)}) copy-start(f32[128,256]{1,0:T(8,128)} %param.51) | copy-start | bytes 393220
  491.9 288.5 %copy-start.23 = (f32[128,1152]{1,0:T(8,128)S(1)}, f32[128,1152]{1,0:T(8,128)}, u32[]{:S(2)}) copy-start(f32[128,1152]{1,0:T(8,128)} %param.60) | copy-start | bytes 1769476
  492.0 288.5 %copy-start.24 = (f32[128,1152]{1,0:T(8,128)S(1)}, f32[128,1152]{1,0:T(8,128)}, u32[]{:S(2)}) copy-start(f32[128,1152]{1,0:T(8,128)} %param.61) | copy-start | bytes 1769476
  492.0 387.7 %copy-start.25 = (f32[128,1152]{1,0:T(8,128)S(1)}, f32[128,1152]{1,0:T(8,128)}, u32[]{:S(2)}) copy-start(f32[128,1152]{1,0:T(8,128)} %param.62) | copy-start | bytes 1769476
  492.0 387.7 %copy-start.26 = (f32[128,1152]{1,0:T(8,128)S(1)}, f32[128,1152]{1,0:T(8,128)}, u32[]{:S(2)}) copy-start(f32[128,1152]{1,0:T(8,128)} %param.63) | copy-start | bytes 1769476
  617.0 362.5 %copy-start.27 = (f32[1152,128]{1,0:T(8,128)S(1)}, f32[1152,128]{1,0:T(8,128)}, u32[]{:S(2)}) copy-start(f32[1152,128]{1,0:T(8,128)} %param.64) | copy-start | bytes 1769476
  783.1 487.6 %copy-start.33 = (f32[2048]{0:T(1024)S(1)}, f32[2048]{0:T(1024)}, u32[]{:S(2)}) copy-start(f32[2048]{0:T(1024)} %copy-done.32) | copy-start | bytes 24580
  783.1 487.6 %copy-start.36 = (f32[1024]{0:T(1024)S(1)}, f32[1024]{0:T(1024)}, u32[]{:S(2)}) copy-start(f32[1024]{0:T(1024)} %param.36) | copy-start | bytes 12292
  1270.7 6.5 copy-start.3
  1277.2 54.6 %copy-start.42 = (bf16[3,256]{1,0:T(4,128)(2,1)S(1)}, bf16[3,256]{1,0:T(4,128)(2,1)}, u32[]{:S(2)}) copy-start(bf16[3,256]{1,0:T(4,128)(2,1)} %param.40) | copy-start | bytes 4612
  1277.2 54.6 %copy-start.49 = (f32[3,256]{1,0:T(4,128)S(1)}, f32[3,256]{1,0:T(4,128)}, u32[]{:S(2)}) copy-start(f32[3,256]{1,0:T(4,128)} %param.54) | copy-start | bytes 9220
  1277.2 54.6 %copy-start.50 = (f32[3,256]{1,0:T(4,128)S(1)}, f32[3,256]{1,0:T(4,128)}, u32[]{:S(2)}) copy-start(f32[3,256]{1,0:T(4,128)} %param.55) | copy-start | bytes 9220
  1277.2 55.2 %copy-start.43 = (f32[1024]{0:T(1024)S(1)}, f32[1024]{0:T(1024)}, u32[]{:S(2)}) copy-start(f32[1024]{0:T(1024)} %param.58) | copy-start | bytes 12292
  1277.3 55.2 %copy-start.44 = (f32[1024]{0:T(1024)S(1)}, f32[1024]{0:T(1024)}, u32[]{:S(2)}) copy-start(f32[1024]{0:T(1024)} %param.59) | copy-start | bytes 12292
  1277.3 55.2 %copy-start.45 = (f32[1024]{0:T(1024)S(1)}, f32[1024]{0:T(1024)}, u32[]{:S(2)}) copy-start(f32[1024]{0:T(1024)} %param.47) | copy-start | bytes 12292
  1277.3 55.2 %copy-start.46 = (f32[1024]{0:T(1024)S(1)}, f32[1024]{0:T(1024)}, u32[]{:S(2)}) copy-start(f32[1024]{0:T(1024)} %param.46) | copy-start | bytes 12292
  1331.8 1.3 copy-start.47
  1331.8 1.3 copy-start.48
  1331.8 1.3 copy-start.51
  (1 other events, 0.6 us)
Sparse Core Ops, SparseCore 0:
  30.8 154.9 all-reduce.9
  245.2 152.9 all-reduce.11
  418.0 64.0 reduce-scatter.13
  486.3 62.4 reduce-scatter.9
  552.6 62.4 reduce-scatter.11
  619.4 62.5 reduce-scatter.7
  686.2 94.2 reduce-scatter.15
  784.6 95.0 reduce-scatter.17
  884.0 95.4 reduce-scatter.19
  982.0 288.6 all-reduce.13
where the time goes:
time: 1350 us; the launch traced here: 1340 us
  waiting for transfers between devices  1070 us (79%)
  matrix products  126 us (9%)
  other arithmetic  66.7 us (5%)
  blocking collectives  37.1 us (3%)
  between operations  15.7 us (1%)
    psum x1, waiting for transfers between devices, body(): lax.psum(jnp.dot(act, w_down, preferred_element_type=jnp.float32), 'tp')  288 us
    psum x1, waiting for transfers between devices, body(): lax.psum(jnp.dot(gated, w_output, preferred_element_type=jnp.float32), 'tp')  155 us
    psum x1, waiting for transfers between devices, body(): dhtwo = lax.psum(dhtwo_part, 'tp')  153 us
    reduce_scatter x1, waiting for transfers between devices, body(): lax.psum_scatter(grad_down, 'seq', scatter_dimension=1, tiled=True)  97.1 us
    reduce_scatter x1, waiting for transfers between devices, body(): lax.psum_scatter(grad_upw, 'seq', scatter_dimension=0, tiled=True)  96.6 us
    reduce_scatter x1, waiting for transfers between devices, body(): lax.psum_scatter(grad_gate, 'seq', scatter_dimension=0, tiled=True)  96.6 us
    reduce_scatter x1, waiting for transfers between devices, body(): lax.psum_scatter(grad_bw, 'seq', scatter_dimension=0, tiled=True)  65 us
    reduce_scatter x1, waiting for transfers between devices, body(): lax.psum_scatter(grad_xw, 'seq', scatter_dimension=0, tiled=True)  64.6 us
  transfers between devices with their start and end apart: 12, of which 11 were waited for; matrix products, arithmetic and copies ran while one was open for 6% of the time, Pallas kernels for 0%

commit v1 on v0

--- a/solution.py
+++ b/solution.py
@@ -97,7 +97,8 @@
     sigma = jax.nn.sigmoid(gate)
     silu_gate = gate * sigma
     act = (silu_gate * upval).astype(jnp.bfloat16)
-    ffn = lax.psum(jnp.dot(act, w_down, preferred_element_type=jnp.float32), "tp")
+    panel = jnp.dot(act, w_down, preferred_element_type=jnp.float32)
+    ffn = jnp.sum(jax.lax.all_gather(panel, axis_name="tp"), 0)
     block_out = (resid + ffn).astype(jnp.bfloat16)
     gout = cotangent.astype(jnp.float32)
     grad_down = inner_rows(act, cotangent)

time: 1350 us -> 1390 us (1.030)
  waiting for transfers between devices: 1070 us -> 1100 us
  other arithmetic: 66.7 us -> 85.8 us
    all_gather x0 -> x1, waiting for transfers between devices: none -> 196 us  [body(): ffn = jnp.sum(jax.lax.all_gather(panel, axis_name='tp'), 0)]
    psum x1, waiting for transfers between devices: 288 us -> 153 us  [body(): dhone = lax.psum(dhone_part, 'tp')]
    reduce_scatter x1, waiting for transfers between devices: 96.6 us -> 28.8 us  [body(): lax.psum_scatter(grad_gate, 'seq', scatter_dimension=0, tiled=True)]
    reduce_scatter x1, waiting for transfers between devices: 0.02 us -> 64.6 us  [body(): lax.psum_scatter(grad_outw, 'seq', scatter_dimension=1, tiled=True)]
    psum x1, waiting for transfers between devices: 153 us -> 112 us  [body(): dhtwo = lax.psum(dhtwo_part, 'tp')]
    reduce_sum x0 -> x1, other arithmetic: none -> 17 us  [body(): ffn = jnp.sum(jax.lax.all_gather(panel, axis_name='tp'), 0)]
  transfers between devices with their start and end apart: 12 -> 13, of which waited for: 11 -> 13; matrix products, arithmetic and copies ran while one was open for 6% -> 9% of each run, Pallas kernels for 0% -> 0%
where the time goes in v1:
time: 1390 us; the launch traced here: 1380 us
  waiting for transfers between devices  1100 us (79%)
  matrix products  127 us (9%)
  other arithmetic  85.8 us (6%)
  blocking collectives  37.1 us (3%)
  between operations  15.4 us (1%)
    all_gather x1, waiting for transfers between devices, body(): ffn = jnp.sum(jax.lax.all_gather(panel, axis_name='tp'), 0)  196 us
    psum x1, waiting for transfers between devices, body(): lax.psum(jnp.dot(gated, w_output, preferred_element_type=jnp.float32), 'tp')  155 us
    psum x1, waiting for transfers between devices, body(): dhone = lax.psum(dhone_part, 'tp')  153 us
    psum x1, waiting for transfers between devices, body(): dhtwo = lax.psum(dhtwo_part, 'tp')  112 us
    reduce_scatter x1, waiting for transfers between devices, body(): lax.psum_scatter(grad_down, 'seq', scatter_dimension=1, tiled=True)  97 us
    reduce_scatter x1, waiting for transfers between devices, body(): lax.psum_scatter(grad_upw, 'seq', scatter_dimension=0, tiled=True)  96.4 us
    reduce_scatter x1, waiting for transfers between devices, body(): lax.psum_scatter(grad_cw, 'seq', scatter_dimension=0, tiled=True)  65.1 us
    reduce_scatter x1, waiting for transfers between devices, body(): lax.psum_scatter(grad_bw, 'seq', scatter_dimension=0, tiled=True)  65.1 us
  transfers between devices with their start and end apart: 13, of which 13 were waited for; matrix products, arithmetic and copies ran while one was open for 9% of the time, Pallas kernels for 0%

profile of v1, /device:TPU:0, one launch (start us, length us, event | category | flops | bytes accessed | tf_op | source)
XLA Modules:
  0.0 1384.1 jit_solution(11439404424124710429)
XLA Ops:
  7.3 3.2 fusion.11
  10.7 1.1 fusion.5
  11.9 1.3 fusion.53
  13.3 2.6 fusion.52
  15.9 4.8 collective-permute-start
  21.5 0.6 collective-permute-done
  22.1 3.7 multiply_convert_fusion.7
  25.8 4.7 fusion.54
  30.7 154.8 %all-reduce.9.cloned.1.call-done = f32[2048,1024]{1,0:T(8,128)} async-done(((f32[2048,1024]{1,0:T(8,128)}), f32[2048,1024]{1,0:T(8,128)}) %all-reduce.9.cloned.1.call-update) | async-done | bytes 8388624 | tf_op jit(solution)/shard_map/psum | solution.py:90
  185.5 5.7 multiply_reduce_fusion.2
  191.3 0.9 multiply_convert_fusion.3
  192.2 2.7 copy-done.1
  194.9 7.9 fusion.56
  202.8 7.9 fusion.55
  210.7 17.9 %multiply_convert_fusion = (bf16[2048,1152]{1,0:T(8,128)(2,1)}, bf16[2048,1152]{1,0:T(8,128)(2,1)}, bf16[2048,1152]{1,0:T(8,128)(2,1)}) fusion(f32[2048,1152]{1,0:T(8,128)} %fusion.55, f32[2048,1152]{1,0:T(8,128)} %fusion.56, bf16[2048,1024]{1,0:T(8,128)(2,1)} %param.34, bf16[1152,1024]{1,0:T(8,128)(2,1)} %param.45), kind=kOutput, calls=%fused_computation.7 | convolution fusion | flops 4867227648 | bytes 39583744 | tf_op jit(solution)/shard_map/dot_general | solution.py:22
  228.6 7.7 fusion.58
  236.3 8.5 convolution_add_fusion
  244.9 10.1 fusion.57
  255.1 10.4 fusion.64
  265.6 10.3 fusion.65
  276.0 9.8 fusion.66
  285.9 112.1 %all-reduce.11.cloned.1.call-done = f32[2048,1024]{1,0:T(8,128)} async-done(((f32[2048,1024]{1,0:T(8,128)}), f32[2048,1024]{1,0:T(8,128)}) %all-reduce.11.cloned.1.call-update) | async-done | bytes 8388624 | tf_op jit(solution)/shard_map/psum | solution.py:111
  398.0 7.3 multiply_reduce_fusion
  405.3 195.9 %all-gather.3.cloned.1.call-done = f32[8192,1024]{1,0:T(8,128)} async-done(((f32[2048,1024]{1,0:T(8,128)}), f32[8192,1024]{1,0:T(8,128)}) %all-gather.3.cloned.1.call-update) | async-done | bytes 33554448 | tf_op jit(solution)/shard_map/all_gather | solution.py:101
  601.2 17.0 %reduce_sum.92 = f32[2048,1024]{1,0:T(8,128)} reduce(f32[4,2048,1024]{2,1,0:T(8,128)} %bitcast.48, f32[]{:T(128)} %constant.28.clone.1), dimensions={0}, to_apply=%region_3.0 | reduce | flops 6291456 | bytes 41943044 | tf_op jit(solution)/shard_map/reduce_sum | solution.py:101
  618.3 13.0 multiply_add_fusion
  631.2 3.4 copy-done
  634.6 2.3 fusion.13
  637.0 4.9 fusion.15
  641.9 0.4 copy-done.17
  642.3 2.2 multiply_reduce_fusion.5
  644.5 0.8 copy-done.4
  645.3 2.3 fusion.62
  647.7 0.5 broadcast_multiply_fusion.2
  648.3 1.6 collective-permute-start.1
  649.8 0.4 pad_add_fusion
  650.2 3.8 collective-permute-done.1
  654.0 0.5 multiply_convert_fusion.4
  654.6 1.6 copy-done.5
  656.2 2.3 fusion.63
  658.8 4.5 fusion.61
  663.4 2.4 fusion.60
  665.8 1.3 fusion.59
  667.1 4.7 add_add_fusion
  671.8 28.8 %reduce-scatter.16.cloned.1.call-done = f32[128,1152]{1,0:T(8,128)} async-done(((f32[1024,1152]{1,0:T(8,128)}), f32[128,1152]{1,0:T(8,128)}) %reduce-scatter.16.cloned.1.call-update) | async-done | bytes 589840 | tf_op jit(solution)/shard_map/reduce_scatter | solution.py:144
  700.6 2.6 convert_subtract_fusion.2
  703.3 96.4 %reduce-scatter.18.cloned.1.call-done = f32[128,1152]{1,0:T(8,128)} async-done(((f32[1024,1152]{1,0:T(8,128)}), f32[128,1152]{1,0:T(8,128)}) %reduce-scatter.18.cloned.1.call-update) | async-done | bytes 589840 | tf_op jit(solution)/shard_map/reduce_scatter | solution.py:145
  799.7 2.6 convert_subtract_fusion.1
  802.4 97.0 %reduce-scatter.20.cloned.1.call-done = f32[1152,128]{1,0:T(8,128)} async-done(((f32[1152,1024]{1,0:T(8,128)}), f32[1152,128]{1,0:T(8,128)}) %reduce-scatter.20.cloned.1.call-update) | async-done | bytes 589840 | tf_op jit(solution)/shard_map/reduce_scatter | solution.py:146
  899.4 3.0 convert_subtract_fusion
  902.4 64.6 %reduce-scatter.14.cloned.1.call-done = f32[256,128]{1,0:T(8,128)} async-done(((f32[256,1024]{1,0:T(8,128)}), f32[256,128]{1,0:T(8,128)}) %reduce-scatter.14.cloned.1.call-update) | async-done | bytes 131088 | tf_op jit(solution)/shard_map/reduce_scatter | solution.py:143
  967.0 1.7 convert_subtract_fusion.3
  968.8 65.1 %reduce-scatter.10.cloned.1.call-done = f32[128,256]{1,0:T(8,128)} async-done(((f32[1024,256]{1,0:T(8,128)}), f32[128,256]{1,0:T(8,128)}) %reduce-scatter.10.cloned.1.call-update) | async-done | bytes 131088 | tf_op jit(solution)/shard_map/reduce_scatter | solution.py:141
  1033.9 1.7 convert_subtract_fusion.5
  1035.6 64.8 %reduce-scatter.12.cloned.1.call-done = f32[128,256]{1,0:T(8,128)} async-done(((f32[1024,256]{1,0:T(8,128)}), f32[128,256]{1,0:T(8,128)}) %reduce-scatter.12.cloned.1.call-update) | async-done | bytes 131088 | tf_op jit(solution)/shard_map/reduce_scatter | solution.py:142
  1100.4 1.7 convert_subtract_fusion.4
  1102.1 65.1 %reduce-scatter.8.cloned.1.call-done = f32[128,256]{1,0:T(8,128)} async-done(((f32[1024,256]{1,0:T(8,128)}), f32[128,256]{1,0:T(8,128)}) %reduce-scatter.8.cloned.1.call-update) | async-done | bytes 131088 | tf_op jit(solution)/shard_map/reduce_scatter | solution.py:140
  1167.2 1.7 convert_subtract_fusion.6
  1169.0 152.6 %all-reduce.13.cloned.1.call-done = f32[2048,1024]{1,0:T(8,128)} async-done(((f32[2048,1024]{1,0:T(8,128)}), f32[2048,1024]{1,0:T(8,128)}) %all-reduce.13.cloned.1.call-update) | async-done | bytes 8388624 | tf_op jit(solution)/shard_map/psum | solution.py:151
  1321.6 5.8 fusion.10
  1327.4 37.1 %all-reduce.4 = (f32[1024]{0:T(1024)S(1)}, f32[3,256]{1,0:T(4,128)S(1)}, f32[1024]{0:T(1024)S(1)}) all-reduce(f32[1024]{0:T(1024)S(1)} %get-tuple-element.44, f32[3,256]{1,0:T(4,128)S(1)} %pad_maximum_fusion.1, f32[1024]{0:T(1024)S(1)} %get-tuple-element.42), channel_id=1, replica_groups=mesh['seq'=8,'tp'=4] {'seq'}, use_global_device_ids=true, to_apply=%region_9.0 | all-reduce | flops 2816 | bytes 22528 | tf_op jit(solution)/shard_map/psum | solution.py:154
  1364.5 0.6 multiply_subtract_fusion.1
  1365.2 0.6 multiply_subtract_fusion
  1365.8 11.6 fusion.9
  (150 shorter events, 1.6 us)
Async XLA Ops:
  7.2 3.3 copy-start.36
  7.2 178.3 %all-reduce.9.cloned.1.call-start = ((), (), s32[]{:S(2)}) async-start(), calls=%async_computation.7 | async-start | bytes 16777216 | tf_op jit(solution)/shard_map/psum | solution.py:90
  7.3 3.5 copy-start.2
  11.9 10.2 copy-start.3
  13.3 7.5 copy-start.42
  13.3 8.8 copy-start.18
  15.9 9.8 copy-start.6
  15.9 6.1 collective-permute-start
  20.8 5.0 copy-start.46
  20.8 4.9 copy-start.48
  20.8 4.9 copy-start.50
  22.1 3.7 copy-start.44
  22.1 3.7 copy-start.13
  30.5 160.8 %copy-start.35 = (f32[1024]{0:T(1024)S(1)}, f32[1024]{0:T(1024)}, u32[]{:S(2)}) copy-start(f32[1024]{0:T(1024)} %param.42) | copy-start | bytes 12292
  30.5 367.5 %all-reduce.11.cloned.1.call-start = ((), (), s32[]{:S(2)}) async-start(), calls=%async_computation.8 | async-start | bytes 16777216 | tf_op jit(solution)/shard_map/psum | solution.py:111
  191.2 3.7 copy-start.1
  191.3 3.6 copy-start.40
  194.9 7.9 copy-start.12
  194.9 7.9 copy-start.38
  210.7 17.9 %copy-start.39 = (bf16[1024,1152]{1,0:T(8,128)(2,1)S(1)}, bf16[1024,1152]{1,0:T(8,128)(2,1)}, u32[]{:S(2)}) copy-start(bf16[1024,1152]{1,0:T(8,128)(2,1)} %param.43) | copy-start | bytes 7077892
  228.6 7.7 copy-start.41
  228.6 7.7 copy-start.61
  244.8 356.4 %all-gather.3.cloned.1.call-start = ((), (), s32[]{:S(2)}) async-start(), calls=%async_computation.17 | async-start | bytes 41943040 | tf_op jit(solution)/shard_map/all_gather | solution.py:101
  255.0 445.6 %reduce-scatter.16.cloned.1.call-start = ((), (), s32[]{:S(2)}) async-start(), calls=%async_computation.14 | async-start | bytes 5308416 | tf_op jit(solution)/shard_map/reduce_scatter | solution.py:144
  265.5 534.2 %reduce-scatter.18.cloned.1.call-start = ((), (), s32[]{:S(2)}) async-start(), calls=%async_computation.15 | async-start | bytes 5308416 | tf_op jit(solution)/shard_map/reduce_scatter | solution.py:145
  275.9 623.5 %reduce-scatter.20.cloned.1.call-start = ((), (), s32[]{:S(2)}) async-start(), calls=%async_computation.16 | async-start | bytes 5308416 | tf_op jit(solution)/shard_map/reduce_scatter | solution.py:146
  285.8 681.2 %reduce-scatter.14.cloned.1.call-start = ((), (), s32[]{:S(2)}) async-start(), calls=%async_computation.13 | async-start | bytes 1179648 | tf_op jit(solution)/shard_map/reduce_scatter | solution.py:143
  631.2 3.4 copy-start
  636.9 5.0 copy-start.7
  637.0 5.0 copy-start.45
  637.0 396.9 %reduce-scatter.10.cloned.1.call-start = ((), (), s32[]{:S(2)}) async-start(), calls=%async_computation.11 | async-start | bytes 1179648 | tf_op jit(solution)/shard_map/reduce_scatter | solution.py:141
  637.0 4.9 copy-start.16
  637.0 5.3 copy-start.17
  642.3 3.0 copy-start.4
  647.6 452.8 %reduce-scatter.12.cloned.1.call-start = ((), (), s32[]{:S(2)}) async-start(), calls=%async_computation.12 | async-start | bytes 1179648 | tf_op jit(solution)/shard_map/reduce_scatter | solution.py:142
  648.2 5.8 copy-start.9
  648.2 5.8 copy-start.10
  648.3 5.8 collective-permute-start.1
  658.5 508.6 %reduce-scatter.8.cloned.1.call-start = ((), (), s32[]{:S(2)}) async-start(), calls=%async_computation.10 | async-start | bytes 1179648 | tf_op jit(solution)/shard_map/reduce_scatter | solution.py:140
  663.3 658.3 %all-reduce.13.cloned.1.call-start = ((), (), s32[]{:S(2)}) async-start(), calls=%async_computation.9 | async-start | bytes 16777216 | tf_op jit(solution)/shard_map/psum | solution.py:151
  671.8 28.8 %copy-start.21 = (f32[128,1152]{1,0:T(8,128)S(1)}, f32[128,1152]{1,0:T(8,128)}, u32[]{:S(2)}) copy-start(f32[128,1152]{1,0:T(8,128)} %param.60) | copy-start | bytes 1769476
  671.8 28.8 %copy-start.22 = (f32[128,1152]{1,0:T(8,128)S(1)}, f32[128,1152]{1,0:T(8,128)}, u32[]{:S(2)}) copy-start(f32[128,1152]{1,0:T(8,128)} %param.61) | copy-start | bytes 1769476
  671.8 128.0 %copy-start.23 = (f32[128,1152]{1,0:T(8,128)S(1)}, f32[128,1152]{1,0:T(8,128)}, u32[]{:S(2)}) copy-start(f32[128,1152]{1,0:T(8,128)} %param.62) | copy-start | bytes 1769476
  671.8 128.0 %copy-start.24 = (f32[128,1152]{1,0:T(8,128)S(1)}, f32[128,1152]{1,0:T(8,128)}, u32[]{:S(2)}) copy-start(f32[128,1152]{1,0:T(8,128)} %param.63) | copy-start | bytes 1769476
  703.3 263.8 %copy-start.25 = (f32[256,128]{1,0:T(8,128)S(1)}, f32[256,128]{1,0:T(8,128)}, u32[]{:S(2)}) copy-start(f32[256,128]{1,0:T(8,128)} %param.56) | copy-start | bytes 393220
  703.3 263.8 %copy-start.26 = (f32[256,128]{1,0:T(8,128)S(1)}, f32[256,128]{1,0:T(8,128)}, u32[]{:S(2)}) copy-start(f32[256,128]{1,0:T(8,128)} %param.57) | copy-start | bytes 393220
  703.3 330.6 %copy-start.27 = (f32[128,256]{1,0:T(8,128)S(1)}, f32[128,256]{1,0:T(8,128)}, u32[]{:S(2)}) copy-start(f32[128,256]{1,0:T(8,128)} %param.50) | copy-start | bytes 393220
  703.3 330.6 %copy-start.28 = (f32[128,256]{1,0:T(8,128)S(1)}, f32[128,256]{1,0:T(8,128)}, u32[]{:S(2)}) copy-start(f32[128,256]{1,0:T(8,128)} %param.51) | copy-start | bytes 393220
  703.3 397.1 %copy-start.29 = (f32[128,256]{1,0:T(8,128)S(1)}, f32[128,256]{1,0:T(8,128)}, u32[]{:S(2)}) copy-start(f32[128,256]{1,0:T(8,128)} %param.52) | copy-start | bytes 393220
  703.3 397.1 %copy-start.30 = (f32[128,256]{1,0:T(8,128)S(1)}, f32[128,256]{1,0:T(8,128)}, u32[]{:S(2)}) copy-start(f32[128,256]{1,0:T(8,128)} %param.53) | copy-start | bytes 393220
  703.3 463.9 %copy-start.31 = (f32[128,256]{1,0:T(8,128)S(1)}, f32[128,256]{1,0:T(8,128)}, u32[]{:S(2)}) copy-start(f32[128,256]{1,0:T(8,128)} %param.48) | copy-start | bytes 393220
  703.3 463.9 %copy-start.32 = (f32[128,256]{1,0:T(8,128)S(1)}, f32[128,256]{1,0:T(8,128)}, u32[]{:S(2)}) copy-start(f32[128,256]{1,0:T(8,128)} %param.49) | copy-start | bytes 393220
  802.4 519.2 %copy-start.34 = (f32[2048]{0:T(1024)S(1)}, f32[2048]{0:T(1024)}, u32[]{:S(2)}) copy-start(f32[2048]{0:T(1024)} %copy-done.33) | copy-start | bytes 24580
  802.4 519.2 %copy-start.37 = (f32[1024]{0:T(1024)S(1)}, f32[1024]{0:T(1024)}, u32[]{:S(2)}) copy-start(f32[1024]{0:T(1024)} %param.36) | copy-start | bytes 12292
  1168.9 195.6 %copy-start.43 = (bf16[3,256]{1,0:T(4,128)(2,1)S(1)}, bf16[3,256]{1,0:T(4,128)(2,1)}, u32[]{:S(2)}) copy-start(bf16[3,256]{1,0:T(4,128)(2,1)} %param.40) | copy-start | bytes 4612
  1168.9 195.6 %copy-start.58 = (f32[3,256]{1,0:T(4,128)S(1)}, f32[3,256]{1,0:T(4,128)}, u32[]{:S(2)}) copy-start(f32[3,256]{1,0:T(4,128)} %param.54) | copy-start | bytes 9220
  1168.9 195.6 %copy-start.59 = (f32[3,256]{1,0:T(4,128)S(1)}, f32[3,256]{1,0:T(4,128)}, u32[]{:S(2)}) copy-start(f32[3,256]{1,0:T(4,128)} %param.55) | copy-start | bytes 9220
  1168.9 196.2 %copy-start.52 = (f32[1024]{0:T(1024)S(1)}, f32[1024]{0:T(1024)}, u32[]{:S(2)}) copy-start(f32[1024]{0:T(1024)} %param.58) | copy-start | bytes 12292
  1168.9 196.2 %copy-start.53 = (f32[1024]{0:T(1024)S(1)}, f32[1024]{0:T(1024)}, u32[]{:S(2)}) copy-start(f32[1024]{0:T(1024)} %param.59) | copy-start | bytes 12292
  1169.0 196.2 %copy-start.54 = (f32[1024]{0:T(1024)S(1)}, f32[1024]{0:T(1024)}, u32[]{:S(2)}) copy-start(f32[1024]{0:T(1024)} %param.47) | copy-start | bytes 12292
  1169.0 196.2 %copy-start.55 = (f32[1024]{0:T(1024)S(1)}, f32[1024]{0:T(1024)}, u32[]{:S(2)}) copy-start(f32[1024]{0:T(1024)} %param.46) | copy-start | bytes 12292
  1364.5 12.9 copy-start.56
  1364.5 12.9 copy-start.57
  1364.5 12.9 copy-start.60
  (11 other events, 21.7 us)
Sparse Core Ops, SparseCore 0:
  30.6 154.8 all-reduce.8
  244.9 152.9 all-reduce.10
  399.5 201.6 all-gather.2
  605.3 95.2 reduce-scatter.15
  704.7 95.0 reduce-scatter.17
  803.8 95.5 reduce-scatter.19
  903.4 63.6 reduce-scatter.13
  971.4 62.4 reduce-scatter.9
  1037.9 62.4 reduce-scatter.11
  1104.6 62.5 reduce-scatter.7
  1169.6 151.8 all-reduce.12
